TPU v7x, 32 devices: a whole 2x2x4 slice. The times are simulated.
32 devices in a mesh: blk: 8 (over y, x, core), replica: 4 (over z).
Axes of the slice: x: 2, y: 2, z: 4, core: 2. Of those that a mesh axis runs over, the one named last changes fastest.
Arguments:
- tokens: bfloat16 [160, 4096], P('blk', 'replica'), may hold values from -6 to 6
- cotangent: bfloat16 [160, 4096], P('blk', 'replica'), may hold values from -6 to 6
- gate_weight: bfloat16 [4096, 28672], P('replica', 'blk'), may hold values from -36 to 36, as said below
- up_weight: bfloat16 [4096, 28672], P('replica', 'blk'), may hold values from -36 to 36, as said below
- down_weight: bfloat16 [28672, 4096], P('blk', 'replica'), may hold values from -72 to 72, as said below
- gate_gain: float32 [28672], P('blk'), may hold values from 0.25 to 1.75
- up_gain: float32 [28672], P('blk'), may hold values from 0.25 to 1.75
- down_gain: float32 [4096], P('replica'), may hold values from 0.25 to 1.75
Outputs:
- grad_tokens: float32 [160, 4096], P('blk', 'replica')
- grad_gate: float32 [4096, 28672], P('replica', 'blk')
- grad_up: float32 [4096, 28672], P('replica', 'blk')
- grad_down: float32 [28672, 4096], P('blk', 'replica')
- grad_gate_gain: float32 [28672], P('blk')
- grad_up_gain: float32 [28672], P('blk')
- grad_down_gain: float32 [4096], P('replica')
Inputs may be any that keep to these rules, and one draw needn't show every extreme that they name: `gate_weight`: real-valued raw weights. `up_weight`: real-valued raw weights. `down_weight`: real-valued raw weights.
All inputs are finite; a program needn't handle non-finite values.
Results may differ from a plain program's by a relative error of at most 0.033.
Values may be sent and summed in bfloat16 or wider, within the bound.
A program may use at most 128 MiB of HBM per device.

v0:
```python
import jax
import jax.numpy as jnp
from jax import lax
from jax.sharding import PartitionSpec as P

epsilon = 0.0001
branch_scale = 0.5


def contract_first(left, right):
    return lax.dot_general(
        left, right, (((0,), (0,)), ((), ())), preferred_element_type=jnp.float32
    )


def contract_last(left, right):
    return lax.dot_general(
        left, right, (((1,), (1,)), ((), ())), preferred_element_type=jnp.float32
    )


def weight_grad(grad_hat, gain, cent, scale, summed, crossed, count):
    grad = scale * (gain * grad_hat - gain * summed / count) - scale * scale * scale * cent * (
        gain * crossed
    )
    return (grad, scale * crossed)


def gating(gate, up, dhidden):
    act = jax.nn.silu(gate)
    hidden = (act * up).astype(jnp.bfloat16)
    sig = jax.nn.sigmoid(gate)
    d_gate = (dhidden * up * sig * (1.0 + gate * (1.0 - sig))).astype(jnp.bfloat16)
    d_up = (dhidden * act).astype(jnp.bfloat16)
    return (d_gate, d_up, hidden)


def local(tokens, cotangent, gate_weight, up_weight, down_weight, gate_gain, up_gain, down_gain):
    width_all = gate_weight.shape[0] * lax.axis_size("replica")
    hidden_all = down_weight.shape[0] * lax.axis_size("blk")
    gate_raw = gate_weight.astype(jnp.float32)
    up_raw = up_weight.astype(jnp.float32)
    down_raw = down_weight.astype(jnp.float32)
    gate_sum, gate_power, up_sum, up_power = lax.psum(
        (
            jnp.sum(gate_raw, axis=0),
            jnp.sum(gate_raw * gate_raw, axis=0),
            jnp.sum(up_raw, axis=0),
            jnp.sum(up_raw * up_raw, axis=0),
        ),
        "replica",
    )
    gate_mean = gate_sum / width_all
    up_mean = up_sum / width_all
    gate_cent = gate_raw - gate_mean
    up_cent = up_raw - up_mean
    gate_square = gate_power - gate_sum * gate_mean
    up_square = up_power - up_sum * up_mean
    down_sum, down_power = lax.psum(
        (jnp.sum(down_raw, axis=0), jnp.sum(down_raw * down_raw, axis=0)), "blk"
    )
    down_mean = down_sum / hidden_all
    down_cent = down_raw - down_mean
    down_square = down_power - down_sum * down_mean
    gate_scale = lax.rsqrt(gate_square + epsilon)
    up_scale = lax.rsqrt(up_square + epsilon)
    down_scale = lax.rsqrt(down_square + epsilon)
    gate_hat = (gate_gain * gate_cent * gate_scale).astype(jnp.bfloat16)
    up_hat = (up_gain * up_cent * up_scale).astype(jnp.bfloat16)
    down_hat = (down_gain * down_cent * down_scale).astype(jnp.bfloat16)
    scaled = (branch_scale * cotangent.astype(jnp.float32)).astype(jnp.bfloat16)
    whole_tokens, whole_scaled = (
        lax.all_gather(tokens, "blk", axis=0, tiled=True),
        lax.all_gather(scaled, "blk", axis=0, tiled=True),
    )
    gate_part = jnp.dot(whole_tokens, gate_hat, preferred_element_type=jnp.float32).astype(
        jnp.bfloat16
    )
    up_part = jnp.dot(whole_tokens, up_hat, preferred_element_type=jnp.float32).astype(jnp.bfloat16)
    down_part = contract_last(whole_scaled, down_hat).astype(jnp.bfloat16)
    gate, up, dhidden = (
        lax.psum(gate_part, "replica").astype(jnp.float32),
        lax.psum(up_part, "replica").astype(jnp.float32),
        lax.psum(down_part, "replica").astype(jnp.float32),
    )
    d_gate, d_up, hidden = gating(gate, up, dhidden)
    share = lax.psum_scatter(
        (contract_last(d_gate, gate_hat) + contract_last(d_up, up_hat)).astype(jnp.bfloat16),
        "blk",
        scatter_dimension=0,
        tiled=True,
    ).astype(jnp.float32)
    grad_tokens = cotangent.astype(jnp.float32) + share
    p_gate = contract_first(whole_tokens, d_gate)
    p_up = contract_first(whole_tokens, d_up)
    p_down = contract_first(hidden, whole_scaled)
    gate_psum, gate_pcross, up_psum, up_pcross = lax.psum(
        (
            jnp.sum(p_gate, axis=0),
            jnp.sum(p_gate * gate_cent, axis=0),
            jnp.sum(p_up, axis=0),
            jnp.sum(p_up * up_cent, axis=0),
        ),
        "replica",
    )
    down_psum, down_pcross = lax.psum(
        (jnp.sum(p_down, axis=0), jnp.sum(p_down * down_cent, axis=0)), "blk"
    )
    grad_gate, grad_gate_gain = weight_grad(
        p_gate, gate_gain, gate_cent, gate_scale, gate_psum, gate_pcross, width_all
    )
    grad_up, grad_up_gain = weight_grad(
        p_up, up_gain, up_cent, up_scale, up_psum, up_pcross, width_all
    )
    grad_down, grad_down_gain = weight_grad(
        p_down, down_gain, down_cent, down_scale, down_psum, down_pcross, hidden_all
    )
    return (
        grad_tokens,
        grad_gate,
        grad_up,
        grad_down,
        grad_gate_gain,
        grad_up_gain,
        grad_down_gain,
    )


def solution(mesh):
    return jax.shard_map(
        local,
        mesh=mesh,
        in_specs=(
            P("blk", "replica"),
            P("blk", "replica"),
            P("replica", "blk"),
            P("replica", "blk"),
            P("blk", "replica"),
            P("blk"),
            P("blk"),
            P("replica"),
        ),
        out_specs=(
            P("blk", "replica"),
            P("replica", "blk"),
            P("replica", "blk"),
            P("blk", "replica"),
            P("blk"),
            P("blk"),
            P("replica"),
        ),
        check_vma=False,
    )
```

profile of v0, /device:TPU:1, one launch (start us, length us, event | category | flops | bytes accessed | tf_op | source)
XLA Modules:
  0.0 367.3 jit_solution(14207939260722395788)
XLA Ops:
  7.2 0.0 all-reduce.11.cloned.1.call-start
  7.2 0.0 copy-start
  7.2 6.5 %convert_reduce_fusion = (f32[3584]{0:T(1024)S(1)}, f32[3584]{0:T(1024)}) fusion(bf16[1024,3584]{1,0:T(8,128)(2,1)} %param.10), kind=kLoop, calls=%fused_computation.2 | loop fusion | flops 14672896 | bytes 7368704 | tf_op jit(solution)/shard_map/reduce_sum | solution.py:46
  13.7 3.3 convert_reduce_fusion.1
  17.0 10.9 %all-gather.1 = bf16[8,20,1024]{2,1,0:T(8,128)(2,1)S(1)} all-gather(bf16[1,20,1024]{2,1,0:T(8,128)(2,1)S(1)} %bitcast.40), channel_id=1, replica_groups=mesh['blk'=8,'replica'=4] {'blk'}, dimensions={0}, use_global_device_ids=true | all-gather | bytes 368640 | tf_op jit(solution)/shard_map/all_gather | solution.py:73
  27.9 0.8 reshape.35
  28.7 16.8 %all-reduce.4 = (f32[3584]{0:T(1024)S(1)}, f32[3584]{0:T(1024)S(1)}, f32[3584]{0:T(1024)S(1)}, f32[3584]{0:T(1024)S(1)}) all-reduce(f32[3584]{0:T(1024)} %get-tuple-element.13, f32[3584]{0:T(1024)} %get-tuple-element.12, f32[3584]{0:T(1024)} %get-tuple-element.11, ...), channel_id=1, replica_groups=mesh['blk'=8,'replica'=4] {'replica'}, use_global_device_ids=true, to_apply=%region_8.0 | all-reduce | flops 14336 | bytes 114688 | tf_op jit(solution)/shard_map/psum | solution.py:44
  45.5 0.6 multiply_multiply_fusion
  46.1 0.0 copy-start.4
  46.2 7.0 %fusion.40 = bf16[160,3584]{1,0:T(8,128)(2,1)} fusion(bf16[160,1024]{1,0:T(8,128)(2,1)} %reshape.35, bf16[1024,3584]{1,0:T(8,128)(2,1)} %param.11, f32[3584]{0:T(1024)S(1)} %get-tuple-element.30, f32[3584]{0:T(1024)S(1)} %get-tuple-element.40, f32[3584]{0:T(1024)} %param.14), kind=kOutput, calls=%fused_computation.49 | convolution fusion | flops 1193328640 | bytes 8857600 | tf_op jit(solution)/shard_map/dot_general | solution.py:79
  53.2 3.8 %fusion.41 = bf16[160,3584]{1,0:T(8,128)(2,1)} fusion(bf16[160,1024]{1,0:T(8,128)(2,1)S(1)} %copy-done.1, bf16[1024,3584]{1,0:T(8,128)(2,1)S(1)} %bitcast.37, f32[3584]{0:T(1024)S(1)} %get-tuple-element.52, f32[3584]{0:T(1024)S(1)} %get-tuple-element.50, f32[3584]{0:T(1024)S(1)} %copy-done.4), kind=kOutput, calls=%fused_computation.50 | convolution fusion | flops 1193328640 | bytes 8857600 | tf_op jit(solution)/shard_map/dot_general | solution.py:76
  57.0 0.0 all-reduce.11.cloned.1.call-update
  57.0 0.2 all-reduce.9.cloned.1.call-start
  57.3 13.3 %all-gather = bf16[8,20,1024]{2,1,0:T(8,128)(2,1)S(1)} all-gather(bf16[1,20,1024]{2,1,0:T(8,128)(2,1)S(1)} %fusion.66), channel_id=1, replica_groups=mesh['blk'=8,'replica'=4] {'blk'}, dimensions={0}, use_global_device_ids=true | all-gather | bytes 368640 | tf_op jit(solution)/shard_map/all_gather | solution.py:74
  70.6 0.1 reshape.33
  70.7 1.2 dynamic-slice.4
  72.6 4.2 %convert_reduce_fusion.2 = f32[1024]{0:T(1024)S(1)} fusion(bf16[3584,1024]{1,0:T(8,128)(2,1)} %param.12), kind=kLoop, calls=%fused_computation.8 | loop fusion | flops 7339008 | bytes 7344128 | tf_op jit(solution)/shard_map/reduce_sum | solution.py:60
  76.8 11.7 %psum.105 = f32[1024]{0:T(1024)S(1)} all-reduce(f32[1024]{0:T(1024)S(1)} %convert_reduce_fusion.2), channel_id=1, replica_groups=mesh['blk'=8,'replica'=4] {'blk'}, use_global_device_ids=true, to_apply=%region_1.0 | all-reduce | flops 1024 | bytes 8192 | tf_op jit(solution)/shard_map/psum | solution.py:59
  88.5 63.1 %all-reduce.11.cloned.1.call-done = (bf16[160,3584]{1,0:T(8,128)(2,1)}, bf16[160,3584]{1,0:T(8,128)(2,1)}) async-done(((bf16[160,3584]{1,0:T(8,128)(2,1)}, bf16[160,3584]{1,0:T(8,128)(2,1)}), (bf16[160,3584]{1,0:T(8,128)(2,1)}, bf16[160,3584]{1,0:T(8,128)(2,1)})) %all-reduce.11.cloned.1.call-update) | async-done | bytes 2293776 | tf_op jit(solution)/shard_map/psum | solution.py:83
  151.6 11.6 %fusion.74 = (f32[1024]{0:T(1024)S(1)}, f32[1024]{0:T(1024)S(1)}, f32[1024]{0:T(1024)S(1)}, f32[3584,1024]{1,0:T(8,128)}) fusion(f32[1024]{0:T(1024)S(1)} %broadcast_multiply_fusion.2, bf16[3584,1024]{1,0:T(8,128)(2,1)} %param.12, bf16[160,1024]{1,0:T(8,128)(2,1)S(1)} %reshape.33, bf16[160,3584]{1,0:T(8,128)(2,1)} %get-tuple-element.25, ...), kind=kOutput, calls=%fused_computation.90 | convolution fusion | flops 1204679680 | bytes 24657920 | tf_op jit(solution)/shard_map/dot_general | solution.py:11
  163.2 21.5 %all-reduce.2 = (f32[1024]{0:T(1024)S(1)}, f32[1024]{0:T(1024)S(1)}, f32[1024]{0:T(1024)S(1)}) all-reduce(f32[1024]{0:T(1024)S(1)} %get-tuple-element.9, f32[1024]{0:T(1024)S(1)} %get-tuple-element.8, f32[1024]{0:T(1024)S(1)} %get-tuple-element.7), channel_id=1, replica_groups=mesh['blk'=8,'replica'=4] {'blk'}, use_global_device_ids=true, to_apply=%region_3.0 | all-reduce | flops 3072 | bytes 24576 | tf_op jit(solution)/shard_map/psum | solution.py:59
  184.7 0.6 multiply_multiply_fusion.5
  185.3 7.0 %fusion.37 = bf16[160,3584]{1,0:T(8,128)(2,1)} fusion(bf16[160,1024]{1,0:T(8,128)(2,1)S(1)} %reshape.33, bf16[3584,1024]{1,0:T(8,128)(2,1)} %param.12, f32[1024]{0:T(1024)S(1)} %get-tuple-element.44, f32[1024]{0:T(1024)S(1)} %broadcast_multiply_fusion.2, f32[1024]{0:T(1024)S(1)} %copy-done.19), kind=kOutput, calls=%fused_computation.46 | convolution fusion | flops 1193328640 | bytes 8826880 | tf_op jit(solution)/shard_map/dot_general | solution.py:17
  192.3 0.0 all-reduce.9.cloned.1.call-update
  192.3 13.4 %fusion.23 = f32[3584,1024]{1,0:T(8,128)} fusion(bf16[3584,1024]{1,0:T(8,128)(2,1)} %param.12, f32[3584,1024]{1,0:T(8,128)} %get-tuple-element.45, f32[1024]{0:T(1024)S(1)} %get-tuple-element.42, f32[1024]{0:T(1024)S(1)} %multiply_multiply_fusion.4, f32[1024]{0:T(1024)S(1)} %get-tuple-element.41, f32[1024]{0:T(1024)S(1)} %get-tuple-element.44, ...), kind=kLoop, calls=%fused_computation.31 | loop fusion | flops 29360128 | bytes 36724736 | tf_op jit(solution)/shard_map/sub | solution.py:23
  205.8 41.6 %all-reduce.9.cloned.1.call-done = bf16[160,3584]{1,0:T(8,128)(2,1)} async-done(((bf16[160,3584]{1,0:T(8,128)(2,1)}), bf16[160,3584]{1,0:T(8,128)(2,1)}) %all-reduce.9.cloned.1.call-update) | async-done | bytes 1146896 | tf_op jit(solution)/shard_map/psum | solution.py:84
  247.4 6.9 %fusion.42 = f32[160,1024]{1,0:T(8,128)S(1)} fusion(bf16[1024,3584]{1,0:T(8,128)(2,1)} %param.11, f32[3584]{0:T(1024)S(1)} %get-tuple-element.30, f32[3584]{0:T(1024)S(1)} %copy-done.11, f32[3584]{0:T(1024)S(1)} %copy-done.7, bf16[160,3584]{1,0:T(8,128)(2,1)} %all-reduce.9.cloned.1.call-done, bf16[160,3584]{1,0:T(8,128)(2,1)S(1)} %copy-done.22), kind=kOutput, calls=%fused_computation.51 | convolution fusion | flops 1197342720 | bytes 10332160 | tf_op jit(solution)/shard_map/dot_general | solution.py:17
  254.3 6.1 %fusion.60 = bf16[160,1024]{1,0:T(8,128)(2,1)S(1)} fusion(f32[160,1024]{1,0:T(8,128)S(1)} %fusion.42, bf16[1024,3584]{1,0:T(8,128)(2,1)} %param.10, f32[3584]{0:T(1024)S(1)} %get-tuple-element.52, f32[3584]{0:T(1024)S(1)} %copy-done.14, f32[3584]{0:T(1024)S(1)} %copy-done.5, bf16[160,3584]{1,0:T(8,128)(2,1)S(1)} %copy-done.23, ...), kind=kOutput, calls=%fused_computation.69 | convolution fusion | flops 1200537600 | bytes 11806720 | tf_op jit(solution)/shard_map/dot_general | solution.py:17
  260.4 15.5 %fusion = bf16[24,1024]{1,0:T(8,128)(2,1)S(1)} fusion(bf16[160,1024]{1,0:T(8,128)(2,1)S(1)} %fusion.60), kind=kCustom, calls=%all-reduce-scatter | all-reduce-scatter fusion | flops 196609 | bytes 377344
  276.0 0.6 slice
  276.6 2.6 collective-permute-start
  279.2 5.0 %collective-permute-start.1 = (bf16[4,1024]{1,0:T(4,128)(2,1)}, bf16[4,1024]{1,0:T(4,128)(2,1)}, u32[]{:S(2)}, u32[]{:S(2)}) collective-permute-start(bf16[4,1024]{1,0:T(4,128)(2,1)} %slice), channel_id=1, source_target_pairs={{0,8},{4,12},{8,16},{12,20},{16,24},{20,28},{1,9},{5,13},{9,17},{1... | collective-permute-start | bytes 24584
  284.2 10.6 %fusion.14 = (f32[3584]{0:T(1024)}, f32[3584,1024]{0,1:T(8,128)}) fusion(bf16[1024,3584]{1,0:T(8,128)(2,1)} %param.10, f32[3584]{0:T(1024)S(1)} %copy-done.14, bf16[160,1024]{1,0:T(8,128)(2,1)S(1)} %copy-done.1, bf16[160,3584]{1,0:T(8,128)(2,1)S(1)} %copy-done.23, bf16[160,3584]{1,0:T(8,128)(2,1)} %all-reduce.9.cloned.1.call-done, ...), kind=kOutput, calls=%fused_computation.22 | convolution fusion | flops 1196536320 | bytes 25817088 | tf_op jit(solution)/shard_map/dot_general | solution.py:11
  294.8 6.6 %reduce_sum.114 = f32[3584]{0:T(1024)} reduce(f32[3584,1024]{0,1:T(8,128)} %get-tuple-element.47, f32[]{:T(128)} %constant.16.clone.1), dimensions={1}, to_apply=%region_16.17 | reduce | flops 3666432 | bytes 14694404 | tf_op jit(solution)/shard_map/reduce_sum | solution.py:99
  301.3 9.3 %fusion.19 = (f32[3584]{0:T(1024)}, f32[3584,1024]{0,1:T(8,128)}) fusion(bf16[1024,3584]{1,0:T(8,128)(2,1)} %param.11, f32[3584]{0:T(1024)S(1)} %copy-done.11, bf16[160,1024]{1,0:T(8,128)(2,1)S(1)} %copy-done.1, bf16[160,3584]{1,0:T(8,128)(2,1)S(1)} %copy-done.25, bf16[160,3584]{1,0:T(8,128)(2,1)S(1)} %copy-done.22), kind=kOutput, calls=%fused_computation.27 | convolution fusion | flops 1193669120 | bytes 24670208 | tf_op jit(solution)/shard_map/dot_general | solution.py:11
  310.7 0.0 slice-start.6
  310.7 6.0 %reduce_sum.116 = f32[3584]{0:T(1024)S(1)} reduce(f32[3584,1024]{0,1:T(8,128)} %get-tuple-element.49, f32[]{:T(128)} %constant.16.clone.1), dimensions={1}, to_apply=%region_20.21 | reduce | flops 3666432 | bytes 14694404 | tf_op jit(solution)/shard_map/reduce_sum | solution.py:101
  316.8 15.0 %all-reduce.3 = (f32[3584]{0:T(1024)S(1)}, f32[3584]{0:T(1024)S(1)}, f32[3584]{0:T(1024)S(1)}, f32[3584]{0:T(1024)S(1)}) all-reduce(f32[3584]{0:T(1024)S(1)} %copy-done.20, f32[3584]{0:T(1024)S(1)} %copy-done.17, f32[3584]{0:T(1024)S(1)} %copy-done.21, f32[3584]{0:T(1024)S(1)} %reduce_sum.116), channel_id=1, replica_groups=mesh['blk'=8,'replica'=4] {'replica'}, use_global_device_ids=true, to_apply=%region_19.20 | all-reduce | flops 14336 | bytes 114688 | tf_op jit(solution)/shard_map/psum | solution.py:97
  331.7 0.6 fusion.77
  332.4 0.6 fusion.76
  333.0 0.0 slice-start.7
  333.0 14.6 %fusion.13 = f32[1024,3584]{1,0:T(8,128)} fusion(bf16[1024,3584]{1,0:T(8,128)(2,1)} %param.10, f32[3584,1024]{0,1:T(8,128)} %get-tuple-element.47, f32[3584]{0:T(1024)S(1)} %get-tuple-element.37, f32[3584]{0:T(1024)S(1)} %copy-done.16, f32[3584]{0:T(1024)S(1)} %get-tuple-element.38, f32[3584]{0:T(1024)S(1)} %get-tuple-element.52, f32[3584]{0:T(1024)S(1)} %copy-done.15, ...), kind=kLoop, calls=%fused_computation.21 | loop fusion | flops 29360128 | bytes 36786176 | tf_op jit(solution)/shard_map/sub | solution.py:23
  347.7 1.7 slice-done.2
  349.3 0.6 slice-done.3
  349.9 1.2 slice-done.7
  351.2 6.9 %fusion.18 = f32[1024,3584]{1,0:T(8,128)} fusion(bf16[1024,3584]{1,0:T(8,128)(2,1)S(1)} %bitcast.39, f32[3584,1024]{0,1:T(8,128)S(1)} %bitcast.35, f32[3584]{0:T(1024)S(1)} %get-tuple-element.34, f32[3584]{0:T(1024)S(1)} %copy-done.9, f32[3584]{0:T(1024)S(1)} %get-tuple-element.35, f32[3584]{0:T(1024)S(1)} %get-tuple-element.30, f32[3584]{0:T(1024)S(1)} %copy-done.12, ...), kind=kLoop, calls=%fused_computation.26 | loop fusion | flops 29360128 | bytes 36786176 | tf_op jit(solution)/shard_map/sub | solution.py:23
  358.0 1.8 concatenate
  359.8 0.7 convert_add_fusion
  (69 shorter events, 0.2 us)
Async XLA Ops:
  7.2 144.4 %all-reduce.11.cloned.1.call-start = ((), (), s32[]{:S(2)}) async-start(), calls=%async_computation.1 | async-start | bytes 4587520 | tf_op jit(solution)/shard_map/psum | solution.py:83
  7.2 6.5 %copy-start = (bf16[1024,3584]{1,0:T(8,128)(2,1)S(1)}, bf16[1024,3584]{1,0:T(8,128)(2,1)}, u32[]{:S(2)}) copy-start(bf16[1024,3584]{1,0:T(8,128)(2,1)} %param.11) | copy-start | bytes 22020100
  7.2 9.8 %copy-start.18 = (bf16[20,1024]{1,0:T(8,128)(2,1)S(1)}, bf16[20,1024]{1,0:T(8,128)(2,1)}, u32[]{:S(2)}) copy-start(bf16[20,1024]{1,0:T(8,128)(2,1)} %param.8) | copy-start | bytes 122884
  27.9 25.3 %slice-start.4 = ((s8[7340032]{0:T(1024)(128)(4,1)}), s8[3145728]{0:T(1024)(128)(4,1)S(1)}, s32[]{:S(2)}) async-start(s8[7340032]{0:T(1024)(128)(4,1)} %bitcast.36), calls=%async_computation.6 | async-start | bytes 6291456
  46.1 7.0 %copy-start.10 = (f32[3584]{0:T(1024)}, f32[3584]{0:T(1024)S(1)}, u32[]{:S(2)}) copy-start(f32[3584]{0:T(1024)S(1)} %get-tuple-element.40) | copy-start | bytes 43012
  46.1 7.0 %copy-start.13 = (f32[3584]{0:T(1024)}, f32[3584]{0:T(1024)S(1)}, u32[]{:S(2)}) copy-start(f32[3584]{0:T(1024)S(1)} %get-tuple-element.50) | copy-start | bytes 43012
  46.1 7.1 %slice-start.5 = ((s8[7340032]{0:T(1024)(128)(4,1)}), s8[4194304]{0:T(1024)(128)(4,1)S(1)}, s32[]{:S(2)}) async-start(s8[7340032]{0:T(1024)(128)(4,1)} %bitcast.36), calls=%async_computation.7 | async-start | bytes 8388608
  46.1 7.1 %copy-start.1 = (bf16[160,1024]{1,0:T(8,128)(2,1)S(1)}, bf16[160,1024]{1,0:T(8,128)(2,1)}, u32[]{:S(2)}) copy-start(bf16[160,1024]{1,0:T(8,128)(2,1)} %reshape.35) | copy-start | bytes 983044
  46.1 7.1 %copy-start.4 = (f32[3584]{0:T(1024)S(1)}, f32[3584]{0:T(1024)}, u32[]{:S(2)}) copy-start(f32[3584]{0:T(1024)} %param.13) | copy-start | bytes 43012
  53.2 4.1 %copy-start.2 = (bf16[20,1024]{1,0:T(8,128)(2,1)S(1)}, bf16[20,1024]{1,0:T(8,128)(2,1)}, u32[]{:S(2)}) copy-start(bf16[20,1024]{1,0:T(8,128)(2,1)} %param.9) | copy-start | bytes 122884
  57.0 190.3 %all-reduce.9.cloned.1.call-start = ((), (), s32[]{:S(2)}) async-start(), calls=%async_computation | async-start | bytes 2293760 | tf_op jit(solution)/shard_map/psum | solution.py:84
  151.6 33.1 %copy-start.19 = (f32[1024]{0:T(1024)S(1)}, f32[1024]{0:T(1024)}, u32[]{:S(2)}) copy-start(f32[1024]{0:T(1024)} %param.15) | copy-start | bytes 12292
  192.3 55.1 %copy-start.7 = (f32[3584]{0:T(1024)S(1)}, f32[3584]{0:T(1024)}, u32[]{:S(2)}) copy-start(f32[3584]{0:T(1024)} %param.14) | copy-start | bytes 43012
  192.3 55.1 %copy-start.11 = (f32[3584]{0:T(1024)S(1)}, f32[3584]{0:T(1024)}, u32[]{:S(2)}) copy-start(f32[3584]{0:T(1024)} %copy-done.10) | copy-start | bytes 43012
  192.3 55.1 %copy-start.22 = (bf16[160,3584]{1,0:T(8,128)(2,1)S(1)}, bf16[160,3584]{1,0:T(8,128)(2,1)}, u32[]{:S(2)}) copy-start(bf16[160,3584]{1,0:T(8,128)(2,1)} %get-tuple-element.26) | copy-start | bytes 3440644
  205.8 48.6 %copy-start.5 = (f32[3584]{0:T(1024)S(1)}, f32[3584]{0:T(1024)}, u32[]{:S(2)}) copy-start(f32[3584]{0:T(1024)} %param.13) | copy-start | bytes 43012
  205.8 48.6 %copy-start.14 = (f32[3584]{0:T(1024)S(1)}, f32[3584]{0:T(1024)}, u32[]{:S(2)}) copy-start(f32[3584]{0:T(1024)} %copy-done.13) | copy-start | bytes 43012
  205.8 48.6 %copy-start.23 = (bf16[160,3584]{1,0:T(8,128)(2,1)S(1)}, bf16[160,3584]{1,0:T(8,128)(2,1)}, u32[]{:S(2)}) copy-start(bf16[160,3584]{1,0:T(8,128)(2,1)} %get-tuple-element.25) | copy-start | bytes 3440644
  247.4 6.9 %copy-start.24 = (bf16[160,3584]{1,0:T(8,128)(2,1)S(1)}, bf16[160,3584]{1,0:T(8,128)(2,1)}, u32[]{:S(2)}) copy-start(bf16[160,3584]{1,0:T(8,128)(2,1)} %all-reduce.9.cloned.1.call-done) | copy-start | bytes 3440644
  276.6 81.4 %collective-permute-start = (bf16[24,1024]{1,0:T(8,128)(2,1)S(1)}, bf16[24,1024]{1,0:T(8,128)(2,1)}, u32[]{:S(2)}, u32[]{:S(2)}) collective-permute-start(bf16[24,1024]{1,0:T(8,128)(2,1)S(1)} %fusion), channel_id=1, source_target_pairs={{0,4},{4,8},{8,12},{12,16},{16,20},{20,24},{24,28},{1,5},{5,9},{9,... | collective-permute-start | bytes 147464
  279.2 78.9 %collective-permute-start.1 = (bf16[4,1024]{1,0:T(4,128)(2,1)}, bf16[4,1024]{1,0:T(4,128)(2,1)}, u32[]{:S(2)}, u32[]{:S(2)}) collective-permute-start(bf16[4,1024]{1,0:T(4,128)(2,1)} %slice), channel_id=1, source_target_pairs={{0,8},{4,12},{8,16},{12,20},{16,24},{20,28},{1,9},{5,13},{9,17},{1... | collective-permute-start | bytes 24584
  294.8 6.6 %copy-start.25 = (bf16[160,3584]{1,0:T(8,128)(2,1)S(1)}, bf16[160,3584]{1,0:T(8,128)(2,1)}, u32[]{:S(2)}) copy-start(bf16[160,3584]{1,0:T(8,128)(2,1)} %all-reduce.9.cloned.1.call-done) | copy-start | bytes 3440644
  310.7 6.1 %copy-start.17 = (f32[3584]{0:T(1024)S(1)}, f32[3584]{0:T(1024)}, u32[]{:S(2)}) copy-start(f32[3584]{0:T(1024)} %reduce_sum.114) | copy-start | bytes 43012
  310.7 6.1 %copy-start.20 = (f32[3584]{0:T(1024)S(1)}, f32[3584]{0:T(1024)}, u32[]{:S(2)}) copy-start(f32[3584]{0:T(1024)} %get-tuple-element.46) | copy-start | bytes 43012
  310.7 6.1 %copy-start.21 = (f32[3584]{0:T(1024)S(1)}, f32[3584]{0:T(1024)}, u32[]{:S(2)}) copy-start(f32[3584]{0:T(1024)} %get-tuple-element.48) | copy-start | bytes 43012
  310.7 21.1 %copy-start.6 = (f32[3584]{0:T(1024)S(1)}, f32[3584]{0:T(1024)}, u32[]{:S(2)}) copy-start(f32[3584]{0:T(1024)} %param.13) | copy-start | bytes 43012
  310.7 21.7 %copy-start.8 = (f32[3584]{0:T(1024)S(1)}, f32[3584]{0:T(1024)}, u32[]{:S(2)}) copy-start(f32[3584]{0:T(1024)} %param.14) | copy-start | bytes 43012
  310.7 22.3 %copy-start.15 = (f32[3584]{0:T(1024)S(1)}, f32[3584]{0:T(1024)}, u32[]{:S(2)}) copy-start(f32[3584]{0:T(1024)} %copy-done.13) | copy-start | bytes 43012
  310.7 22.3 %copy-start.16 = (f32[3584]{0:T(1024)S(1)}, f32[3584]{0:T(1024)}, u32[]{:S(2)}) copy-start(f32[3584]{0:T(1024)} %get-tuple-element.51) | copy-start | bytes 43012
  310.7 37.0 %slice-start.6 = ((s8[7340032]{0:T(1024)(128)(4,1)}), s8[3145728]{0:T(1024)(128)(4,1)S(1)}, s32[]{:S(2)}) async-start(s8[7340032]{0:T(1024)(128)(4,1)} %bitcast.38), calls=%async_computation.8 | async-start | bytes 6291456
  333.0 14.7 %slice-start = ((s8[14680064]{0:T(1024)(128)(4,1)}), s8[4194304]{0:T(1024)(128)(4,1)S(1)}, s32[]{:S(2)}) async-start(s8[14680064]{0:T(1024)(128)(4,1)} %bitcast.34), calls=%async_computation.2 | async-start | bytes 8388608
  333.0 14.7 %slice-start.1 = ((s8[14680064]{0:T(1024)(128)(4,1)}), s8[4194304]{0:T(1024)(128)(4,1)S(1)}, s32[]{:S(2)}) async-start(s8[14680064]{0:T(1024)(128)(4,1)} %bitcast.34), calls=%async_computation.3 | async-start | bytes 8388608
  333.0 16.4 %slice-start.2 = ((s8[14680064]{0:T(1024)(128)(4,1)}), s8[4194304]{0:T(1024)(128)(4,1)S(1)}, s32[]{:S(2)}) async-start(s8[14680064]{0:T(1024)(128)(4,1)} %bitcast.34), calls=%async_computation.4 | async-start | bytes 8388608
  333.0 17.0 %slice-start.3 = ((s8[14680064]{0:T(1024)(128)(4,1)}), s8[2097152]{0:T(1024)(128)(4,1)S(1)}, s32[]{:S(2)}) async-start(s8[14680064]{0:T(1024)(128)(4,1)} %bitcast.34), calls=%async_computation.5 | async-start | bytes 4194304
  333.0 18.1 %slice-start.7 = ((s8[7340032]{0:T(1024)(128)(4,1)}), s8[4194304]{0:T(1024)(128)(4,1)S(1)}, s32[]{:S(2)}) async-start(s8[7340032]{0:T(1024)(128)(4,1)} %bitcast.38), calls=%async_computation.9 | async-start | bytes 8388608
  333.0 18.1 %copy-start.9 = (f32[3584]{0:T(1024)S(1)}, f32[3584]{0:T(1024)}, u32[]{:S(2)}) copy-start(f32[3584]{0:T(1024)} %get-tuple-element.29) | copy-start | bytes 43012
  333.0 18.1 %copy-start.12 = (f32[3584]{0:T(1024)S(1)}, f32[3584]{0:T(1024)}, u32[]{:S(2)}) copy-start(f32[3584]{0:T(1024)} %copy-done.10) | copy-start | bytes 43012
  351.1 8.6 %copy-start.3 = (bf16[20,1024]{1,0:T(8,128)(2,1)S(1)}, bf16[20,1024]{1,0:T(8,128)(2,1)}, u32[]{:S(2)}) copy-start(bf16[20,1024]{1,0:T(8,128)(2,1)} %param.9) | copy-start | bytes 122884
Sparse Core Ops, SparseCore 0:
  57.2 94.3 all-reduce.10
  192.4 54.9 all-reduce.8
where the time goes:
time: 369 us; the launch traced here: 367 us
  blocking collectives  105 us (28%)
  waiting for transfers between devices  105 us (28%)
  other arithmetic  64.6 us (18%)
  matrix products  62.3 us (17%)
  between operations  15 us (4%)
  local copies, waits for them, and re-layouts  8.08 us (2%)
  starting transfers between devices  7.85 us (2%)
    psum x1, waiting for transfers between devices, local(): lax.psum(up_part, 'replica').astype(jnp.float32)  63.1 us
    psum x1, waiting for transfers between devices, local(): lax.psum(down_part, 'replica').astype(jnp.float32)  41.6 us
    sub x3, other arithmetic, weight_grad(): scale * (gain * grad_hat - gain * summed / count)  34.9 us
    psum x2, blocking collectives, local(): lax.psum((jnp.sum(down_raw, axis=0), jnp.sum(down_raw * down_raw, axis=0)...  33.2 us
    dot_general x3, matrix products, contract_first(): lax.dot_general(left, right, (((0,), (0,)), ((), ())), preferred_element_...  31.6 us
    dot_general x3, matrix products, contract_last(): lax.dot_general(left, right, (((1,), (1,)), ((), ())), preferred_element_...  19.9 us
    psum x1, blocking collectives, local(): lax.psum((jnp.sum(gate_raw, axis=0), jnp.sum(gate_raw * gate_raw, axis=0)...  16.8 us
    unnamed x1, blocking collectives  15.5 us
  transfers between devices with their start and end apart: 4, of which 2 were waited for; matrix products, arithmetic and copies ran while one was open for 20% of the time, Pallas kernels for 0%

commit v1 on v0

v1 whole, which is shorter than its diff:
```python
import jax
import jax.numpy as jnp
from jax import lax
from jax.sharding import PartitionSpec as P

epsilon = 0.0001
branch_scale = 0.5


def contract_first(left, right):
    return lax.dot_general(
        left, right, (((0,), (0,)), ((), ())), preferred_element_type=jnp.float32
    )


def contract_last(left, right):
    return lax.dot_general(
        left, right, (((1,), (1,)), ((), ())), preferred_element_type=jnp.float32
    )


def local(tokens, cotangent, gate_weight, up_weight, down_weight, gate_gain, up_gain, down_gain):
    bf16, f32 = jnp.bfloat16, jnp.float32
    n_blk = lax.axis_size("blk")
    width_all = gate_weight.shape[0] * lax.axis_size("replica")
    hidden_all = down_weight.shape[0] * n_blk
    own, width = tokens.shape
    scaled = (branch_scale * cotangent.astype(f32)).astype(bf16)
    both = lax.all_gather(jnp.stack([tokens, scaled]), "blk", axis=0)
    whole_tokens = both[:, 0].reshape(n_blk * own, width)
    whole_scaled = both[:, 1].reshape(n_blk * own, width)
    token_sum = jnp.sum(whole_tokens.astype(f32), axis=1)

    gate_raw = gate_weight.astype(f32)
    up_raw = up_weight.astype(f32)
    gate_sum, gate_power, up_sum, up_power, token_all = lax.psum(
        (
            jnp.sum(gate_raw, axis=0),
            jnp.sum(gate_raw * gate_raw, axis=0),
            jnp.sum(up_raw, axis=0),
            jnp.sum(up_raw * up_raw, axis=0),
            token_sum,
        ),
        "replica",
    )
    gate_mean = gate_sum / width_all
    up_mean = up_sum / width_all
    gate_scale = lax.rsqrt(gate_power - gate_sum * gate_mean + epsilon)
    up_scale = lax.rsqrt(up_power - up_sum * up_mean + epsilon)
    gate_factor = gate_gain * gate_scale
    up_factor = up_gain * up_scale
    gate_part = (
        gate_factor
        * (
            jnp.dot(whole_tokens, gate_weight, preferred_element_type=f32)
            - token_sum[:, None] * gate_mean
        )
    ).astype(bf16)
    up_part = (
        up_factor
        * (
            jnp.dot(whole_tokens, up_weight, preferred_element_type=f32)
            - token_sum[:, None] * up_mean
        )
    ).astype(bf16)
    gate, up = lax.psum((gate_part, up_part), "replica")

    down_weight, _, _ = lax.optimization_barrier((down_weight, gate_part, up_part))
    down_raw = down_weight.astype(f32)
    down_sum, down_power = lax.psum(
        (jnp.sum(down_raw, axis=0), jnp.sum(down_raw * down_raw, axis=0)), "blk"
    )
    down_mean = down_sum / hidden_all
    down_scale = lax.rsqrt(down_power - down_sum * down_mean + epsilon)
    outward = (whole_scaled.astype(f32) * (down_gain * down_scale)).astype(bf16)
    outward_mean = jnp.sum(outward.astype(f32) * down_mean, axis=1)
    down_part = (contract_last(outward, down_weight) - outward_mean[:, None]).astype(bf16)
    gate, up, down_part = lax.optimization_barrier((gate, up, down_part))
    dhidden = lax.psum(down_part, "replica").astype(f32)
    gate, up = gate.astype(f32), up.astype(f32)

    sig = jax.nn.sigmoid(gate)
    act = gate * sig
    hidden = (act * up).astype(bf16)
    hidden_sum = jnp.sum(hidden.astype(f32), axis=1)
    out_part = (
        jnp.dot(hidden, down_weight, preferred_element_type=f32) - hidden_sum[:, None] * down_mean
    )
    outward32 = outward.astype(f32)
    down_psum, down_cross = lax.psum(
        (
            jnp.sum(hidden_sum[:, None] * outward32, axis=0),
            jnp.sum(outward32 * out_part, axis=0),
        ),
        "blk",
    )
    grad_down_gain = down_cross / down_gain
    down_slope = down_scale * down_scale * down_cross
    grad_down = (
        contract_first(hidden, outward)
        - down_slope * down_raw
        + (down_slope * down_mean - down_psum / hidden_all)
    )
    dhidden, grad_down, gate, up = lax.optimization_barrier((dhidden, grad_down, gate, up))
    sig = jax.nn.sigmoid(gate)
    act = gate * sig
    d_gate = dhidden * up * sig * (1.0 + gate * (1.0 - sig))
    d_up = dhidden * act
    gate_cross = jnp.sum(d_gate * gate, axis=0)
    up_cross = jnp.sum(d_up * up, axis=0)
    gate_back = (d_gate * gate_factor).astype(bf16)
    up_back = (d_up * up_factor).astype(bf16)
    back_mean = jnp.sum(gate_back.astype(f32) * gate_mean + up_back.astype(f32) * up_mean, axis=1)
    back = (
        contract_last(gate_back, gate_weight)
        + contract_last(up_back, up_weight)
        - back_mean[:, None]
    ).astype(bf16)
    pieces = lax.all_to_all(
        back.reshape(n_blk, own, width), "blk", split_axis=0, concat_axis=0, tiled=True
    )
    grad_tokens = cotangent.astype(f32) + jnp.sum(pieces.astype(f32), axis=0)

    grad_gate_gain = gate_cross / gate_gain
    grad_up_gain = up_cross / up_gain
    gate_slope = gate_scale * gate_scale * gate_cross
    up_slope = up_scale * up_scale * up_cross
    gate_psum = jnp.sum(token_all[:, None] * gate_back.astype(f32), axis=0)
    up_psum = jnp.sum(token_all[:, None] * up_back.astype(f32), axis=0)
    grad_gate = (
        contract_first(whole_tokens, gate_back)
        - gate_slope * gate_raw
        + (gate_slope * gate_mean - gate_psum / width_all)
    )
    grad_up = (
        contract_first(whole_tokens, up_back)
        - up_slope * up_raw
        + (up_slope * up_mean - up_psum / width_all)
    )
    return (
        grad_tokens,
        grad_gate,
        grad_up,
        grad_down,
        grad_gate_gain,
        grad_up_gain,
        grad_down_gain,
    )


def solution(mesh):
    return jax.shard_map(
        local,
        mesh=mesh,
        in_specs=(
            P("blk", "replica"),
            P("blk", "replica"),
            P("replica", "blk"),
            P("replica", "blk"),
            P("blk", "replica"),
            P("blk"),
            P("blk"),
            P("replica"),
        ),
        out_specs=(
            P("blk", "replica"),
            P("replica", "blk"),
            P("replica", "blk"),
            P("blk", "replica"),
            P("blk"),
            P("blk"),
            P("replica"),
        ),
        check_vma=False,
    )
```

time: 369 us -> 260 us (0.70)
  blocking collectives: 105 us -> 58.1 us
  other arithmetic: 64.6 us -> 32.3 us
  waiting for transfers between devices: 105 us -> 87 us
  matrix products: 62.3 us -> 57.8 us
    sub x3 -> x2, other arithmetic: 34.9 us -> 1.23 us  [the longest x1 0.63 us: local(): up_slope * up_mean - up_psum / width_all]
    psum x2, waiting for transfers between devices: 105 us -> 87 us  [the longest x1 64.9 us: local(): gate, up = lax.psum((gate_part, up_part), 'replica')]
    psum x2 -> x1, blocking collectives: 33.2 us -> 16.3 us  [local(): lax.psum((jnp.sum(down_raw, axis=0), jnp.sum(down_raw * down_raw, axis=0)...]
    unnamed x1 -> x0, blocking collectives: 15.5 us -> none
    all_gather x2 -> x1, blocking collectives: 24.2 us -> 11.8 us  [local(): both = lax.all_gather(jnp.stack([tokens, scaled]), 'blk', axis=0)]
    unnamed x2 -> x0, starting transfers between devices: 7.59 us -> none
    unnamed x73 -> x44, local copies, waits for them, and re-layouts: 8.08 us -> 1.91 us
    convert_element_type x0 -> x5, other arithmetic: none -> 6.06 us  [the longest x2 3.25 us: local(): gate, up = (gate.astype(f32), up.astype(f32))]
  transfers between devices with their start and end apart: 4 -> 3, of which waited for: 2 -> 2; matrix products, arithmetic and copies ran while one was open for 20% -> 21% of each run, Pallas kernels for 0% -> 0%
where the time goes in v1:
time: 260 us; the launch traced here: 259 us
  waiting for transfers between devices  87 us (33%)
  blocking collectives  58.1 us (22%)
  matrix products  57.8 us (22%)
  other arithmetic  32.3 us (12%)
  between operations  14.4 us (6%)
  local copies, waits for them, and re-layouts  5.77 us (2%)
  starting transfers between devices  4.19 us (2%)
    psum x1, waiting for transfers between devices, local(): gate, up = lax.psum((gate_part, up_part), 'replica')  64.9 us
    dot_general x3, matrix products, contract_first(): lax.dot_general(left, right, (((0,), (0,)), ((), ())), preferred_element_...  29.7 us
    psum x1, waiting for transfers between devices, local(): dhidden = lax.psum(down_part, 'replica').astype(f32)  22.1 us
    psum x1, blocking collectives, local(): lax.psum((jnp.sum(gate_raw, axis=0), jnp.sum(gate_raw * gate_raw, axis=0)...  17.5 us
    psum x1, blocking collectives, local(): lax.psum((jnp.sum(down_raw, axis=0), jnp.sum(down_raw * down_raw, axis=0)...  16.3 us
    dot_general x3, matrix products, contract_last(): lax.dot_general(left, right, (((1,), (1,)), ((), ())), preferred_element_...  15.5 us
    psum x1, blocking collectives, local(): lax.psum((jnp.sum(hidden_sum[:, None] * outward32, axis=0), jnp.sum(outwa...  12.5 us
    all_gather x1, blocking collectives, local(): both = lax.all_gather(jnp.stack([tokens, scaled]), 'blk', axis=0)  11.8 us
  transfers between devices with their start and end apart: 3, of which 2 were waited for; matrix products, arithmetic and copies ran while one was open for 21% of the time, Pallas kernels for 0%

profile of v1, /device:TPU:1, one launch (start us, length us, event | category | flops | bytes accessed | tf_op | source)
XLA Modules:
  0.0 259.5 jit_solution(1719394744202527683)
XLA Ops:
  7.2 0.0 all-reduce.9.cloned.1.call-start
  7.2 0.8 fusion.26
  8.0 0.8 pad_maximum_fusion
  8.8 11.8 %all-gather = bf16[16,20,1024]{2,1,0:T(8,128)(2,1)S(1)} all-gather(bf16[2,20,1024]{2,1,0:T(8,128)(2,1)S(1)} %pad_maximum_fusion), channel_id=2, replica_groups=mesh['blk'=8,'replica'=4] {'blk'}, dimensions={0}, use_global_device_ids=true | all-gather | bytes 737280 | tf_op jit(solution)/shard_map/all_gather | solution.py:29
  20.6 0.1 convert_reduce_fusion.5
  20.8 0.7 copy-done.1
  21.5 1.1 fusion.24
  22.6 5.9 %convert_reduce_fusion.2 = (f32[3584]{0:T(1024)S(1)}, f32[3584]{0:T(1024)S(1)}) fusion(bf16[1024,3584]{1,0:T(8,128)(2,1)} %param.10), kind=kLoop, calls=%fused_computation.7 | loop fusion | flops 14672896 | bytes 7368704 | tf_op jit(solution)/shard_map/reduce_sum | solution.py:38
  28.5 2.6 %fusion.3 = (f32[3584]{0:T(1024)S(1)}, f32[3584]{0:T(1024)S(1)}) fusion(bf16[1024,3584]{1,0:T(8,128)(2,1)S(1)} %copy-done), kind=kLoop, calls=%fused_computation.12 | loop fusion | flops 14672896 | bytes 7368704 | tf_op jit(solution)/shard_map/reduce_sum | solution.py:41
  31.2 0.6 mul.250
  31.8 1.2 reshape_squeeze.4
  33.0 17.5 %all-reduce.2 = (f32[3584]{0:T(1024)}, f32[3584]{0:T(1024)}, f32[3584]{0:T(1024)}, f32[3584]{0:T(1024)}, f32[160]{0:T(256)}) all-reduce(f32[3584]{0:T(1024)S(1)} %get-tuple-element.28, f32[3584]{0:T(1024)S(1)} %get-tuple-element.27, f32[3584]{0:T(1024)S(1)} %get-tuple-element.26, ...), channel_id=1, replica_groups=mesh['blk'=8,'replica'=4] {'replica'}, use_global_device_ids=true, to_apply=%region_1.0 | all-reduce | flops 14496 | bytes 115968 | tf_op jit(solution)/shard_map/psum | solution.py:36
  50.6 0.7 fusion.27
  51.3 0.8 fusion.28
  52.1 5.6 %fusion.12 = bf16[160,3584]{1,0:T(8,128)(2,1)} fusion(bf16[160,1024]{1,0:T(8,128)(2,1)S(1)} %reshape_squeeze.4, bf16[1024,3584]{1,0:T(8,128)(2,1)} %param.11, f32[3584]{0:T(1024)S(1)} %get-tuple-element.67, f32[3584]{0:T(1024)S(1)} %get-tuple-element.66, f32[160]{0:T(256)} %mul.250), kind=kOutput, calls=%fused_computation.24 | convolution fusion | flops 1176698880 | bytes 8843904 | tf_op jit(solution)/shard_map/dot_general | solution.py:62
  57.7 2.4 fusion.11
  60.1 0.0 all-reduce.9.cloned.1.call-update
  60.1 0.0 all-reduce.7.cloned.1.call-start
  60.2 1.1 copy-done.5
  61.3 0.1 reshape.64
  61.3 5.1 %convert_reduce_fusion = (f32[1024]{0:T(1024)S(1)}, f32[1024]{0:T(1024)S(1)}) fusion(bf16[3584,1024]{1,0:T(8,128)(2,1)} %param.12), kind=kLoop, calls=%fused_computation.1 | loop fusion | flops 14678016 | bytes 7348224 | tf_op jit(solution)/shard_map/reduce_sum | solution.py:71
  66.5 16.3 %all-reduce.1 = (f32[1024]{0:T(1024)S(1)}, f32[1024]{0:T(1024)S(1)}) all-reduce(f32[1024]{0:T(1024)S(1)} %get-tuple-element.24, f32[1024]{0:T(1024)S(1)} %get-tuple-element.23), channel_id=1, replica_groups=mesh['blk'=8,'replica'=4] {'blk'}, use_global_device_ids=true, to_apply=%region_12.0 | all-reduce | flops 2048 | bytes 16384 | tf_op jit(solution)/shard_map/psum | solution.py:70
  82.8 0.2 fusion.22
  83.0 0.1 sub.62
  83.1 0.1 multiply_convert_fusion.4
  83.1 6.7 %fusion.13 = bf16[160,3584]{1,0:T(8,128)(2,1)} fusion(bf16[160,1024]{1,0:T(8,128)(2,1)S(1)} %multiply_convert_fusion.4, bf16[3584,1024]{1,0:T(8,128)(2,1)} %param.12, f32[160]{0:T(256)S(1)} %sub.62), kind=kOutput, calls=%fused_computation.25 | convolution fusion | flops 1175552000 | bytes 8815232 | tf_op jit(solution)/shard_map/dot_general | solution.py:17
  89.8 64.9 %all-reduce.9.cloned.1.call-done = (bf16[160,3584]{1,0:T(8,128)(2,1)}, bf16[160,3584]{1,0:T(8,128)(2,1)}) async-done(((bf16[160,3584]{1,0:T(8,128)(2,1)}, bf16[160,3584]{1,0:T(8,128)(2,1)}), (bf16[160,3584]{1,0:T(8,128)(2,1)}, bf16[160,3584]{1,0:T(8,128)(2,1)})) %all-reduce.9.cloned.1.call-update) | async-done | bytes 2293776 | tf_op jit(solution)/shard_map/psum | solution.py:66
  154.8 2.6 %convert_reduce_fusion.3 = (f32[160]{0:T(256)S(1)}, bf16[160,3584]{1,0:T(8,128)(2,1)S(1)}) fusion(bf16[160,3584]{1,0:T(8,128)(2,1)} %get-tuple-element.18, bf16[160,3584]{1,0:T(8,128)(2,1)} %get-tuple-element.17), kind=kLoop, calls=%fused_computation.41 | loop fusion | flops 5734240 | bytes 3441280 | tf_op jit(solution)/shard_map/reduce_sum | solution.py:85
  157.4 0.1 mul.282
  157.4 4.6 %fusion.21 = f32[1024]{0:T(1024)S(1)} fusion(bf16[160,3584]{1,0:T(8,128)(2,1)S(1)} %get-tuple-element.54, bf16[3584,1024]{1,0:T(8,128)(2,1)} %param.12, bf16[160,1024]{1,0:T(8,128)(2,1)S(1)} %multiply_convert_fusion.4, f32[1024]{0:T(1024)S(1)} %get-tuple-element.69, f32[160]{0:T(256)S(1)} %get-tuple-element.53), kind=kOutput, calls=%fused_computation.48 | convolution fusion | flops 1175223296 | bytes 8823424 | tf_op jit(solution)/shard_map/dot_general | solution.py:87
  162.0 0.2 fusion.23
  162.2 1.6 convert_element_type.105
  163.8 1.6 convert_element_type.106
  165.5 12.5 %all-reduce = (f32[1024]{0:T(1024)S(1)}, f32[1024]{0:T(1024)S(1)}) all-reduce(f32[1024]{0:T(1024)S(1)} %fusion.23, f32[1024]{0:T(1024)S(1)} %fusion.21), channel_id=1, replica_groups=mesh['blk'=8,'replica'=4] {'blk'}, use_global_device_ids=true, to_apply=%region_21.0 | all-reduce | flops 2048 | bytes 16384 | tf_op jit(solution)/shard_map/psum | solution.py:90
  177.9 0.6 multiply_subtract_fusion.2
  178.5 10.8 %fusion.8 = f32[3584,1024]{1,0:T(8,128)} fusion(bf16[3584,1024]{1,0:T(8,128)(2,1)} %param.12, bf16[160,3584]{1,0:T(8,128)(2,1)S(1)} %get-tuple-element.54, bf16[160,1024]{1,0:T(8,128)(2,1)S(1)} %multiply_convert_fusion.4, f32[1024]{0:T(1024)S(1)} %get-tuple-element.51, f32[1024]{0:T(1024)S(1)} %get-tuple-element.52), kind=kOutput, calls=%fused_computation.17 | convolution fusion | flops 1189085184 | bytes 23502848 | tf_op jit(solution)/shard_map/dot_general | solution.py:11
  189.4 22.1 %all-reduce.7.cloned.1.call-done = bf16[160,3584]{1,0:T(8,128)(2,1)} async-done(((bf16[160,3584]{1,0:T(8,128)(2,1)}), bf16[160,3584]{1,0:T(8,128)(2,1)}) %all-reduce.7.cloned.1.call-update) | async-done | bytes 1146896 | tf_op jit(solution)/shard_map/psum | solution.py:79
  211.5 1.6 convert_element_type.104
  213.2 4.4 %multiply_reduce_fusion = (f32[3584]{0:T(1024)S(1)}, f32[3584]{0:T(1024)S(1)}, f32[3584]{0:T(1024)S(1)}, f32[160]{0:T(256)S(1)}, bf16[160,3584]{1,0:T(8,128)(2,1...) fusion(f32[160,3584]{1,0:T(8,128)} %convert_element_type.106, f32[160,3584]{1,0:T(8,128)S(1)} %convert_element_type.104, ...), kind=kLoop, calls=%fused_computation.34 | loop fusion | flops 16615264 | bytes 9291008 | tf_op jit(solution)/shard_map/reduce_sum | solution.py:110
  217.6 5.6 %fusion.30 = f32[160,1024]{1,0:T(8,128)S(1)} fusion(bf16[160,3584]{1,0:T(8,128)(2,1)S(1)} %get-tuple-element.57, bf16[1024,3584]{1,0:T(8,128)(2,1)} %param.10), kind=kOutput, calls=%fused_computation.80 | convolution fusion | flops 1174405120 | bytes 9142272 | tf_op jit(solution)/shard_map/dot_general | solution.py:17
  223.3 3.2 %fusion.20 = bf16[160,1024]{1,0:T(8,128)(2,1)} fusion(f32[160,1024]{1,0:T(8,128)S(1)} %fusion.30, bf16[160,3584]{1,0:T(8,128)(2,1)S(1)} %get-tuple-element.59, bf16[1024,3584]{1,0:T(8,128)(2,1)S(1)} %bitcast.41, f32[160]{0:T(256)S(1)} %get-tuple-element.56), kind=kOutput, calls=%fused_computation.47 | convolution fusion | flops 1174896640 | bytes 9470592 | tf_op jit(solution)/shard_map/dot_general | solution.py:17
  226.5 1.8 reshape.63
  228.3 4.1 %all-to-all-start = ((bf16[8,20,1024]{2,1,0:T(8,128)(2,1)}), bf16[8,20,1024]{2,1,0:T(8,128)(2,1)S(1)}, u32[]{:S(2)}, u32[]{:S(2)}) async-start(bf16[8,20,1024]{2,1,0:T(8,128)(2,1)} %reshape.63), calls=%async_computation | async-start | bytes 786432 | tf_op jit(solution)/shard_map/all_to_all | solution.py:119
  232.4 0.6 multiply_subtract_fusion
  233.1 10.9 %fusion.5 = f32[1024,3584]{1,0:T(8,128)} fusion(bf16[1024,3584]{1,0:T(8,128)(2,1)} %param.11, bf16[160,1024]{1,0:T(8,128)(2,1)S(1)} %reshape_squeeze.4, bf16[160,3584]{1,0:T(8,128)(2,1)S(1)} %get-tuple-element.59, f32[3584]{0:T(1024)S(1)} %get-tuple-element.45, f32[3584]{0:T(1024)S(1)} %get-tuple-element.46), kind=kOutput, calls=%fused_computation.14 | convolution fusion | flops 1189085184 | bytes 23523328 | tf_op jit(solution)/shard_map/dot_general | solution.py:11
  244.0 7.9 %fusion.2 = f32[1024,3584]{1,0:T(8,128)} fusion(bf16[1024,3584]{1,0:T(8,128)(2,1)S(1)} %bitcast.45, bf16[160,1024]{1,0:T(8,128)(2,1)S(1)} %reshape_squeeze.4, bf16[160,3584]{1,0:T(8,128)(2,1)S(1)} %get-tuple-element.57, f32[3584]{0:T(1024)S(1)} %get-tuple-element.72, f32[3584]{0:T(1024)S(1)} %get-tuple-element.73), kind=kOutput, calls=%fused_computation.11 | convolution fusion | flops 1189085184 | bytes 23523328 | tf_op jit(solution)/shard_map/dot_general | solution.py:11
  251.9 0.1 convert_reduce_fusion.4
  252.0 0.7 convert_add_fusion
  (48 shorter events, 0.1 us)
Async XLA Ops:
  7.2 147.6 %all-reduce.9.cloned.1.call-start = ((), (), s32[]{:S(2)}) async-start(), calls=%async_computation.2 | async-start | bytes 4587520 | tf_op jit(solution)/shard_map/psum | solution.py:66
  20.6 0.9 copy-start.1
  22.6 5.9 %copy-start = (bf16[1024,3584]{1,0:T(8,128)(2,1)S(1)}, bf16[1024,3584]{1,0:T(8,128)(2,1)}, u32[]{:S(2)}) copy-start(bf16[1024,3584]{1,0:T(8,128)(2,1)} %param.11) | copy-start | bytes 22020100
  28.5 22.1 %copy-start.7 = (f32[3584]{0:T(1024)S(1)}, f32[3584]{0:T(1024)}, u32[]{:S(2)}) copy-start(f32[3584]{0:T(1024)} %param.13) | copy-start | bytes 43012
  31.8 25.9 %slice-start.2 = ((s8[7340032]{0:T(1024)(128)(4,1)}), s8[3145728]{0:T(1024)(128)(4,1)S(1)}, s32[]{:S(2)}) async-start(s8[7340032]{0:T(1024)(128)(4,1)} %bitcast.42), calls=%async_computation.5 | async-start | bytes 6291456
  52.1 5.6 %slice-start.3 = ((s8[7340032]{0:T(1024)(128)(4,1)}), s8[4194304]{0:T(1024)(128)(4,1)S(1)}, s32[]{:S(2)}) async-start(s8[7340032]{0:T(1024)(128)(4,1)} %bitcast.42), calls=%async_computation.6 | async-start | bytes 8388608
  52.1 5.6 %copy-start.14 = (f32[160]{0:T(256)S(1)}, f32[160]{0:T(256)}, u32[]{:S(2)}) copy-start(f32[160]{0:T(256)} %mul.250) | copy-start | bytes 1924
  60.1 1.1 copy-start.5
  60.1 151.3 %all-reduce.7.cloned.1.call-start = ((), (), s32[]{:S(2)}) async-start(), calls=%async_computation.1 | async-start | bytes 2293760 | tf_op jit(solution)/shard_map/psum | solution.py:79
  61.3 21.4 %copy-start.13 = (f32[1024]{0:T(1024)S(1)}, f32[1024]{0:T(1024)}, u32[]{:S(2)}) copy-start(f32[1024]{0:T(1024)} %param.15) | copy-start | bytes 12292
  61.3 21.5 %copy-start.2 = (bf16[16,20,1024]{2,1,0:T(8,128)(2,1)S(1)}, bf16[16,20,1024]{2,1,0:T(8,128)(2,1)}, u32[]{:S(2)}) copy-start(bf16[16,20,1024]{2,1,0:T(8,128)(2,1)} %copy-done.1) | copy-start | bytes 1966084
  157.4 4.8 %copy-start.4 = (bf16[160,3584]{1,0:T(8,128)(2,1)S(1)}, bf16[160,3584]{1,0:T(8,128)(2,1)}, u32[]{:S(2)}) copy-start(bf16[160,3584]{1,0:T(8,128)(2,1)} %get-tuple-element.17) | copy-start | bytes 3440644
  162.0 1.8 copy-start.3
  189.4 23.7 %copy-start.15 = (f32[160]{0:T(256)S(1)}, f32[160]{0:T(256)}, u32[]{:S(2)}) copy-start(f32[160]{0:T(256)} %get-tuple-element.42) | copy-start | bytes 1924
  211.5 11.7 %slice-start = ((s8[7340032]{0:T(1024)(128)(4,1)}), s8[4194304]{0:T(1024)(128)(4,1)S(1)}, s32[]{:S(2)}) async-start(s8[7340032]{0:T(1024)(128)(4,1)} %bitcast.40), calls=%async_computation.3 | async-start | bytes 8388608
  213.1 10.1 %slice-start.1 = ((s8[7340032]{0:T(1024)(128)(4,1)}), s8[3145728]{0:T(1024)(128)(4,1)S(1)}, s32[]{:S(2)}) async-start(s8[7340032]{0:T(1024)(128)(4,1)} %bitcast.40), calls=%async_computation.4 | async-start | bytes 6291456
  223.2 9.2 %copy-start.8 = (f32[3584]{0:T(1024)S(1)}, f32[3584]{0:T(1024)}, u32[]{:S(2)}) copy-start(f32[3584]{0:T(1024)} %param.14) | copy-start | bytes 43012
  223.2 9.2 %copy-start.9 = (f32[3584]{0:T(1024)S(1)}, f32[3584]{0:T(1024)}, u32[]{:S(2)}) copy-start(f32[3584]{0:T(1024)} %get-tuple-element.38) | copy-start | bytes 43012
  223.2 9.2 %copy-start.10 = (f32[3584]{0:T(1024)S(1)}, f32[3584]{0:T(1024)}, u32[]{:S(2)}) copy-start(f32[3584]{0:T(1024)} %get-tuple-element.39) | copy-start | bytes 43012
  223.3 9.2 %copy-start.11 = (f32[3584]{0:T(1024)S(1)}, f32[3584]{0:T(1024)}, u32[]{:S(2)}) copy-start(f32[3584]{0:T(1024)} %get-tuple-element.40) | copy-start | bytes 43012
  223.3 9.2 %copy-start.12 = (f32[3584]{0:T(1024)S(1)}, f32[3584]{0:T(1024)}, u32[]{:S(2)}) copy-start(f32[3584]{0:T(1024)} %get-tuple-element.41) | copy-start | bytes 43012
  228.3 23.6 %all-to-all-start = ((bf16[8,20,1024]{2,1,0:T(8,128)(2,1)}), bf16[8,20,1024]{2,1,0:T(8,128)(2,1)S(1)}, u32[]{:S(2)}, u32[]{:S(2)}) async-start(bf16[8,20,1024]{2,1,0:T(8,128)(2,1)} %reshape.63), calls=%async_computation | async-start | bytes 786432 | tf_op jit(solution)/shard_map/all_to_all | solution.py:119
  233.1 10.9 %slice-start.4 = ((s8[7340032]{0:T(1024)(128)(4,1)}), s8[4194304]{0:T(1024)(128)(4,1)S(1)}, s32[]{:S(2)}) async-start(s8[7340032]{0:T(1024)(128)(4,1)} %bitcast.44), calls=%async_computation.7 | async-start | bytes 8388608
  233.1 10.9 %slice-start.5 = ((s8[7340032]{0:T(1024)(128)(4,1)}), s8[3145728]{0:T(1024)(128)(4,1)S(1)}, s32[]{:S(2)}) async-start(s8[7340032]{0:T(1024)(128)(4,1)} %bitcast.44), calls=%async_computation.8 | async-start | bytes 6291456
  244.0 8.0 %copy-start.6 = (bf16[20,1024]{1,0:T(8,128)(2,1)S(1)}, bf16[20,1024]{1,0:T(8,128)(2,1)}, u32[]{:S(2)}) copy-start(bf16[20,1024]{1,0:T(8,128)(2,1)} %param.9) | copy-start | bytes 122884
Sparse Core Ops, SparseCore 0:
  60.3 94.4 all-reduce.8
  157.2 54.2 all-reduce.6

commit v2 on v1

--- a/solution.py
+++ b/solution.py
@@ -19,6 +19,16 @@
     )
 
 
+def shift(left, right):
+    return lax.dot_general(
+        left,
+        right,
+        (((0,), (0,)), ((), ())),
+        precision=lax.Precision.HIGHEST,
+        preferred_element_type=jnp.float32,
+    )
+
+
 def local(tokens, cotangent, gate_weight, up_weight, down_weight, gate_gain, up_gain, down_gain):
     bf16, f32 = jnp.bfloat16, jnp.float32
     n_blk = lax.axis_size("blk")
@@ -33,37 +43,45 @@
 
     gate_raw = gate_weight.astype(f32)
     up_raw = up_weight.astype(f32)
-    gate_sum, gate_power, up_sum, up_power, token_all = lax.psum(
-        (
-            jnp.sum(gate_raw, axis=0),
-            jnp.sum(gate_raw * gate_raw, axis=0),
-            jnp.sum(up_raw, axis=0),
-            jnp.sum(up_raw * up_raw, axis=0),
-            token_sum,
-        ),
-        "replica",
+    block = gate_weight.shape[0]
+    hidden_own = gate_weight.shape[1]
+    sums = (
+        jnp.sum(gate_raw, axis=0),
+        jnp.sum(gate_raw * gate_raw, axis=0),
+        jnp.sum(up_raw, axis=0),
+        jnp.sum(up_raw * up_raw, axis=0),
     )
+    gate_part = (
+        jnp.dot(whole_tokens, gate_weight, preferred_element_type=f32)
+        - token_sum[:, None] * (sums[0] / block)
+    ).astype(bf16)
+    up_part = (
+        jnp.dot(whole_tokens, up_weight, preferred_element_type=f32)
+        - token_sum[:, None] * (sums[2] / block)
+    ).astype(bf16)
+    gate, up = lax.psum((gate_part, up_part), "replica")
+
+    lanes = jnp.concatenate(sums + (token_sum,))
+    lanes = jnp.pad(lanes, (0, -lanes.shape[0] % 1024)).reshape(-1, 128)
+    lanes, _, _ = lax.optimization_barrier((lanes, gate_part, up_part))
+    lanes = lax.all_gather(lanes, "replica", axis=0)
+    stats = lanes.reshape(lanes.shape[0], -1)
+    gate_sums = stats[:, :hidden_own]
+    up_sums = stats[:, 2 * hidden_own : 3 * hidden_own]
+    token_sums = stats[:, 4 * hidden_own : 4 * hidden_own + n_blk * own]
+    gate_power = jnp.sum(stats[:, hidden_own : 2 * hidden_own], axis=0)
+    up_power = jnp.sum(stats[:, 3 * hidden_own : 4 * hidden_own], axis=0)
+    gate_sum = jnp.sum(gate_sums, axis=0)
+    up_sum = jnp.sum(up_sums, axis=0)
+    token_all = jnp.sum(token_sums, axis=0)
     gate_mean = gate_sum / width_all
     up_mean = up_sum / width_all
     gate_scale = lax.rsqrt(gate_power - gate_sum * gate_mean + epsilon)
     up_scale = lax.rsqrt(up_power - up_sum * up_mean + epsilon)
     gate_factor = gate_gain * gate_scale
     up_factor = up_gain * up_scale
-    gate_part = (
-        gate_factor
-        * (
-            jnp.dot(whole_tokens, gate_weight, preferred_element_type=f32)
-            - token_sum[:, None] * gate_mean
-        )
-    ).astype(bf16)
-    up_part = (
-        up_factor
-        * (
-            jnp.dot(whole_tokens, up_weight, preferred_element_type=f32)
-            - token_sum[:, None] * up_mean
-        )
-    ).astype(bf16)
-    gate, up = lax.psum((gate_part, up_part), "replica")
+    gate_shift = shift(token_sums, gate_sums / block - gate_mean)
+    up_shift = shift(token_sums, up_sums / block - up_mean)
 
     down_weight, _, _ = lax.optimization_barrier((down_weight, gate_part, up_part))
     down_raw = down_weight.astype(f32)
@@ -75,9 +93,12 @@
     outward = (whole_scaled.astype(f32) * (down_gain * down_scale)).astype(bf16)
     outward_mean = jnp.sum(outward.astype(f32) * down_mean, axis=1)
     down_part = (contract_last(outward, down_weight) - outward_mean[:, None]).astype(bf16)
-    gate, up, down_part = lax.optimization_barrier((gate, up, down_part))
+    gate, up, down_part, gate_shift, up_shift = lax.optimization_barrier(
+        (gate, up, down_part, gate_shift, up_shift)
+    )
     dhidden = lax.psum(down_part, "replica").astype(f32)
-    gate, up = gate.astype(f32), up.astype(f32)
+    gate = gate_factor * (gate.astype(f32) + gate_shift)
+    up = up_factor * (up.astype(f32) + up_shift)
 
     sig = jax.nn.sigmoid(gate)
     act = gate * sig

time: 260 us -> 244 us (0.938)
  waiting for transfers between devices: 87 us -> 69.6 us
  matrix products: 57.8 us -> 65.4 us
  blocking collectives: 58.1 us -> 51 us
    psum x1 -> x0, blocking collectives: 17.5 us -> none  [local(): lax.psum((jnp.sum(gate_raw, axis=0), jnp.sum(gate_raw * gate_raw, axis=0)...]
    psum x1, waiting for transfers between devices: 64.9 us -> 49.4 us  [local(): gate, up = lax.psum((gate_part, up_part), 'replica')]
    all_gather x0 -> x1, blocking collectives: none -> 14.6 us  [local(): lanes = lax.all_gather(lanes, 'replica', axis=0)]
    dot_general x0 -> x2, matrix products: none -> 7.3 us  [shift(): lax.dot_general(left, right, (((0,), (0,)), ((), ())), precision=lax.Prec...]
    psum x1, blocking collectives: 16.3 us -> 11.9 us  [local(): lax.psum((jnp.sum(down_raw, axis=0), jnp.sum(down_raw * down_raw, axis=0)...]
    reduce_sum x1, other arithmetic: 2.61 us -> 6.45 us  [local(): hidden_sum = jnp.sum(hidden.astype(f32), axis=1)]
    convert_element_type x2 -> x0, other arithmetic: 3.25 us -> none  [local(): gate, up = (gate.astype(f32), up.astype(f32))]
    reduce_sum x1 -> x3, other arithmetic: 5.88 us -> 6.62 us  [the longest x1 5.88 us: local(): jnp.sum(gate_raw * gate_raw, axis=0)]
  transfers between devices with their start and end apart: 3 -> 3, of which waited for: 2 -> 2; matrix products, arithmetic and copies ran while one was open for 21% -> 26% of each run, Pallas kernels for 0% -> 0%
where the time goes in v2:
time: 244 us; the launch traced here: 243 us
  waiting for transfers between devices  69.6 us (29%)
  matrix products  65.4 us (27%)
  blocking collectives  51 us (21%)
  other arithmetic  32.8 us (13%)
  between operations  14.4 us (6%)
  local copies, waits for them, and re-layouts  6.01 us (2%)
  starting transfers between devices  4.19 us (2%)
    psum x1, waiting for transfers between devices, local(): gate, up = lax.psum((gate_part, up_part), 'replica')  49.4 us
    dot_general x3, matrix products, contract_first(): lax.dot_general(left, right, (((0,), (0,)), ((), ())), preferred_element_...  29.7 us
    psum x1, waiting for transfers between devices, local(): dhidden = lax.psum(down_part, 'replica').astype(f32)  20.2 us
    dot_general x3, matrix products, contract_last(): lax.dot_general(left, right, (((1,), (1,)), ((), ())), preferred_element_...  15.5 us
    all_gather x1, blocking collectives, local(): lanes = lax.all_gather(lanes, 'replica', axis=0)  14.6 us
    psum x1, blocking collectives, local(): lax.psum((jnp.sum(hidden_sum[:, None] * outward32, axis=0), jnp.sum(outwa...  12.7 us
    psum x1, blocking collectives, local(): lax.psum((jnp.sum(down_raw, axis=0), jnp.sum(down_raw * down_raw, axis=0)...  11.9 us
    all_gather x1, blocking collectives, local(): both = lax.all_gather(jnp.stack([tokens, scaled]), 'blk', axis=0)  11.8 us
  transfers between devices with their start and end apart: 3, of which 2 were waited for; matrix products, arithmetic and copies ran while one was open for 26% of the time, Pallas kernels for 0%

profile of v2, /device:TPU:1, one launch (start us, length us, event | category | flops | bytes accessed | tf_op | source)
XLA Modules:
  0.0 243.4 jit_solution(773502250850428910)
XLA Ops:
  7.2 0.8 fusion.32
  8.0 0.8 pad_maximum_fusion
  8.9 11.8 %all-gather = bf16[16,20,1024]{2,1,0:T(8,128)(2,1)S(1)} all-gather(bf16[2,20,1024]{2,1,0:T(8,128)(2,1)S(1)} %pad_maximum_fusion), channel_id=2, replica_groups=mesh['blk'=8,'replica'=4] {'blk'}, dimensions={0}, use_global_device_ids=true | all-gather | bytes 737280 | tf_op jit(solution)/shard_map/all_gather | solution.py:39
  20.6 0.1 convert_reduce_fusion.5
  20.8 0.7 copy-done.1
  21.5 1.1 fusion.22
  22.6 5.9 %fusion = (f32[3584]{0:T(1024)S(1)}, f32[3584]{0:T(1024)S(1)}) fusion(bf16[1024,3584]{1,0:T(8,128)(2,1)} %param.10), kind=kLoop, calls=%fused_computation.9 | loop fusion | flops 14672896 | bytes 7368704 | tf_op jit(solution)/shard_map/reduce_sum | solution.py:50
  28.5 2.6 %fusion.3 = (f32[3584]{0:T(1024)S(1)}, f32[3584]{0:T(1024)S(1)}) fusion(bf16[1024,3584]{1,0:T(8,128)(2,1)S(1)} %copy-done), kind=kLoop, calls=%fused_computation.12 | loop fusion | flops 14672896 | bytes 7368704 | tf_op jit(solution)/shard_map/reduce_sum | solution.py:52
  31.2 0.1 mul.300
  31.3 0.6 broadcast_multiply_fusion.2
  31.9 1.2 reshape_squeeze.4
  33.1 5.6 %fusion.10 = bf16[160,3584]{1,0:T(8,128)(2,1)} fusion(bf16[160,1024]{1,0:T(8,128)(2,1)S(1)} %reshape_squeeze.4, bf16[1024,3584]{1,0:T(8,128)(2,1)} %param.11, f32[3584]{0:T(1024)} %get-tuple-element.75, f32[160]{0:T(256)S(1)} %mul.300), kind=kOutput, calls=%fused_computation.22 | convolution fusion | flops 1176125440 | bytes 8829568 | tf_op jit(solution)/shard_map/dot_general | solution.py:59
  38.7 2.4 fusion.9
  41.2 0.0 all-reduce.7.cloned.1.call-start
  41.2 5.1 %convert_reduce_fusion = (f32[1024]{0:T(1024)S(1)}, f32[1024]{0:T(1024)S(1)}) fusion(bf16[3584,1024]{1,0:T(8,128)(2,1)} %param.12), kind=kLoop, calls=%fused_computation.1 | loop fusion | flops 14678016 | bytes 7348224 | tf_op jit(solution)/shard_map/reduce_sum | solution.py:89
  46.4 11.9 %all-reduce.2 = (f32[1024]{0:T(1024)S(1)}, f32[1024]{0:T(1024)S(1)}) all-reduce(f32[1024]{0:T(1024)S(1)} %get-tuple-element.30, f32[1024]{0:T(1024)S(1)} %get-tuple-element.29), channel_id=1, replica_groups=mesh['blk'=8,'replica'=4] {'blk'}, use_global_device_ids=true, to_apply=%region_6.0 | all-reduce | flops 2048 | bytes 16384 | tf_op jit(solution)/shard_map/psum | solution.py:88
  58.4 0.1 reshape.124
  58.5 0.5 copy-done.14
  58.9 0.2 fusion.20
  59.1 0.7 sub.98
  59.8 14.6 %all-gather.1 = f32[480,128]{1,0:T(8,128)S(1)} all-gather(f32[120,128]{1,0:T(8,128)S(1)} %pad_bitcast_fusion), channel_id=3, replica_groups=mesh['blk'=8,'replica'=4] {'replica'}, dimensions={0}, use_global_device_ids=true | all-gather | bytes 307200 | tf_op jit(solution)/shard_map/all_gather | solution.py:67
  74.3 0.1 reshape.122
  74.5 0.6 slice_reduce_fusion.4
  75.1 0.1 slice_reduce_fusion
  75.3 0.1 multiply_convert_fusion.4
  75.4 3.0 %fusion.27 = f32[160,3584]{1,0:T(8,128)S(1)} fusion(f32[4,15360]{1,0:T(4,128)} %copy-done.7, f32[3584]{0:T(1024)S(1)} %get-tuple-element.72), kind=kOutput, calls=%fused_computation.70 | convolution fusion | flops 27553792 | bytes 2369536 | tf_op jit(solution)/shard_map/dot_general | solution.py:23
  78.4 4.3 %fusion.24 = f32[160,3584]{1,0:T(8,128)} fusion(f32[4,15360]{1,0:T(4,128)} %copy-done.7, f32[3584]{0:T(1024)S(1)} %get-tuple-element.74), kind=kOutput, calls=%fused_computation.67 | convolution fusion | flops 27553792 | bytes 2369536 | tf_op jit(solution)/shard_map/dot_general | solution.py:23
  82.7 6.7 %fusion.11 = bf16[160,3584]{1,0:T(8,128)(2,1)} fusion(bf16[160,1024]{1,0:T(8,128)(2,1)S(1)} %multiply_convert_fusion.4, bf16[3584,1024]{1,0:T(8,128)(2,1)} %param.12, f32[160]{0:T(256)S(1)} %copy-done.17), kind=kOutput, calls=%fused_computation.23 | convolution fusion | flops 1175552000 | bytes 8815232 | tf_op jit(solution)/shard_map/dot_general | solution.py:17
  89.4 49.4 %all-reduce.9.cloned.1.call-done = (bf16[160,3584]{1,0:T(8,128)(2,1)}, bf16[160,3584]{1,0:T(8,128)(2,1)}) async-done(((bf16[160,3584]{1,0:T(8,128)(2,1)}, bf16[160,3584]{1,0:T(8,128)(2,1)}), (bf16[160,3584]{1,0:T(8,128)(2,1)}, bf16[160,3584]{1,0:T(8,128)(2,1)})) %all-reduce.9.cloned.1.call-update) | async-done | bytes 2293776 | tf_op jit(solution)/shard_map/psum | solution.py:62
  138.8 6.4 %convert_reduce_fusion.3 = (f32[160]{0:T(256)}, bf16[160,3584]{1,0:T(8,128)(2,1)}, f32[160,3584]{1,0:T(8,128)}, f32[160,3584]{1,0:T(8,128)}) fusion(f32[160,3584]{1,0:T(8,128)S(1)} %fusion.27, bf16[160,3584]{1,0:T(8,128)(2,1)} %get-tuple-element.21, f32[3584]{0:T(1024)S(1)} %get-tuple-element.71, f32[160,3584]{1,0:T(8,128)} %fusion.24, ...), kind=kLoop, calls=%fused_computation.39 | loop fusion | flops 8028000 | bytes 12644992 | tf_op jit(solution)/shard_map/reduce_sum | solution.py:106
  145.2 0.8 mul.336
  146.0 4.9 %fusion.19 = f32[1024]{0:T(1024)S(1)} fusion(bf16[160,3584]{1,0:T(8,128)(2,1)} %get-tuple-element.59, bf16[3584,1024]{1,0:T(8,128)(2,1)} %param.12, bf16[160,1024]{1,0:T(8,128)(2,1)} %copy-done.5, f32[1024]{0:T(1024)S(1)} %get-tuple-element.80, f32[160]{0:T(256)} %get-tuple-element.58), kind=kOutput, calls=%fused_computation.48 | convolution fusion | flops 1175223296 | bytes 8823424 | tf_op jit(solution)/shard_map/dot_general | solution.py:108
  150.9 0.2 fusion.21
  151.1 12.7 %all-reduce.1 = (f32[1024]{0:T(1024)S(1)}, f32[1024]{0:T(1024)S(1)}) all-reduce(f32[1024]{0:T(1024)S(1)} %fusion.21, f32[1024]{0:T(1024)S(1)} %fusion.19), channel_id=1, replica_groups=mesh['blk'=8,'replica'=4] {'blk'}, use_global_device_ids=true, to_apply=%region_21.22 | all-reduce | flops 2048 | bytes 16384 | tf_op jit(solution)/shard_map/psum | solution.py:111
  163.8 0.6 multiply_subtract_fusion.2
  164.4 10.8 %fusion.8 = f32[3584,1024]{1,0:T(8,128)} fusion(bf16[3584,1024]{1,0:T(8,128)(2,1)} %param.12, bf16[160,3584]{1,0:T(8,128)(2,1)S(1)} %copy-done.3, bf16[160,1024]{1,0:T(8,128)(2,1)S(1)} %copy-done.6, f32[1024]{0:T(1024)S(1)} %get-tuple-element.56, f32[1024]{0:T(1024)S(1)} %get-tuple-element.57), kind=kOutput, calls=%fused_computation.17 | convolution fusion | flops 1189085184 | bytes 23502848 | tf_op jit(solution)/shard_map/dot_general | solution.py:11
  175.3 20.2 %all-reduce.7.cloned.1.call-done = bf16[160,3584]{1,0:T(8,128)(2,1)} async-done(((bf16[160,3584]{1,0:T(8,128)(2,1)}), bf16[160,3584]{1,0:T(8,128)(2,1)}) %all-reduce.7.cloned.1.call-update) | async-done | bytes 1146896 | tf_op jit(solution)/shard_map/psum | solution.py:99
  195.5 1.6 convert_element_type.106
  197.1 4.4 %multiply_reduce_fusion = (f32[3584]{0:T(1024)S(1)}, f32[3584]{0:T(1024)S(1)}, f32[3584]{0:T(1024)S(1)}, f32[160]{0:T(256)S(1)}, bf16[160,3584]{1,0:T(8,128)(2,1...) fusion(f32[160,3584]{1,0:T(8,128)} %get-tuple-element.26, f32[160,3584]{1,0:T(8,128)S(1)} %convert_element_type.106, ...), kind=kLoop, calls=%fused_computation.32 | loop fusion | flops 16615264 | bytes 9291008 | tf_op jit(solution)/shard_map/reduce_sum | solution.py:131
  201.6 5.6 %fusion.44 = f32[160,1024]{1,0:T(8,128)S(1)} fusion(bf16[160,3584]{1,0:T(8,128)(2,1)S(1)} %get-tuple-element.64, bf16[1024,3584]{1,0:T(8,128)(2,1)} %param.10), kind=kOutput, calls=%fused_computation.109 | convolution fusion | flops 1174405120 | bytes 9142272 | tf_op jit(solution)/shard_map/dot_general | solution.py:17
  207.2 3.2 %fusion.18 = bf16[160,1024]{1,0:T(8,128)(2,1)} fusion(f32[160,1024]{1,0:T(8,128)S(1)} %fusion.44, bf16[160,3584]{1,0:T(8,128)(2,1)S(1)} %get-tuple-element.66, bf16[1024,3584]{1,0:T(8,128)(2,1)S(1)} %bitcast.43, f32[160]{0:T(256)S(1)} %get-tuple-element.63), kind=kOutput, calls=%fused_computation.47 | convolution fusion | flops 1174896640 | bytes 9470592 | tf_op jit(solution)/shard_map/dot_general | solution.py:17
  210.5 1.8 reshape.123
  212.2 4.1 %all-to-all-start = ((bf16[8,20,1024]{2,1,0:T(8,128)(2,1)}), bf16[8,20,1024]{2,1,0:T(8,128)(2,1)S(1)}, u32[]{:S(2)}, u32[]{:S(2)}) async-start(bf16[8,20,1024]{2,1,0:T(8,128)(2,1)} %reshape.123), calls=%async_computation | async-start | bytes 786432 | tf_op jit(solution)/shard_map/all_to_all | solution.py:140
  216.4 0.6 multiply_subtract_fusion
  217.0 10.9 %fusion.5 = f32[1024,3584]{1,0:T(8,128)} fusion(bf16[1024,3584]{1,0:T(8,128)(2,1)} %param.11, bf16[160,1024]{1,0:T(8,128)(2,1)S(1)} %reshape_squeeze.4, bf16[160,3584]{1,0:T(8,128)(2,1)S(1)} %get-tuple-element.66, f32[3584]{0:T(1024)S(1)} %get-tuple-element.50, f32[3584]{0:T(1024)S(1)} %get-tuple-element.51), kind=kOutput, calls=%fused_computation.14 | convolution fusion | flops 1189085184 | bytes 23523328 | tf_op jit(solution)/shard_map/dot_general | solution.py:11
  228.0 7.9 %fusion.2 = f32[1024,3584]{1,0:T(8,128)} fusion(bf16[1024,3584]{1,0:T(8,128)(2,1)S(1)} %bitcast.47, bf16[160,1024]{1,0:T(8,128)(2,1)S(1)} %reshape_squeeze.4, bf16[160,3584]{1,0:T(8,128)(2,1)S(1)} %get-tuple-element.64, f32[3584]{0:T(1024)S(1)} %get-tuple-element.83, f32[3584]{0:T(1024)S(1)} %get-tuple-element.84), kind=kOutput, calls=%fused_computation.11 | convolution fusion | flops 1189085184 | bytes 23523328 | tf_op jit(solution)/shard_map/dot_general | solution.py:11
  235.9 0.1 convert_reduce_fusion.4
  235.9 0.7 convert_add_fusion
  (62 shorter events, 0.3 us)
Async XLA Ops:
  7.2 131.6 %all-reduce.9.cloned.1.call-start = ((), (), s32[]{:S(2)}) async-start(), calls=%async_computation.2 | async-start | bytes 4587520 | tf_op jit(solution)/shard_map/psum | solution.py:62
  20.6 0.9 copy-start.1
  22.6 5.9 %copy-start = (bf16[1024,3584]{1,0:T(8,128)(2,1)S(1)}, bf16[1024,3584]{1,0:T(8,128)(2,1)}, u32[]{:S(2)}) copy-start(bf16[1024,3584]{1,0:T(8,128)(2,1)} %param.11) | copy-start | bytes 22020100
  31.9 6.9 %slice-start.2 = ((s8[7340032]{0:T(1024)(128)(4,1)}), s8[3145728]{0:T(1024)(128)(4,1)S(1)}, s32[]{:S(2)}) async-start(s8[7340032]{0:T(1024)(128)(4,1)} %bitcast.44), calls=%async_computation.5 | async-start | bytes 6291456
  33.1 5.6 %slice-start.3 = ((s8[7340032]{0:T(1024)(128)(4,1)}), s8[4194304]{0:T(1024)(128)(4,1)S(1)}, s32[]{:S(2)}) async-start(s8[7340032]{0:T(1024)(128)(4,1)} %bitcast.44), calls=%async_computation.6 | async-start | bytes 8388608
  41.1 17.2 %copy-start.13 = (f32[1024]{0:T(1024)S(1)}, f32[1024]{0:T(1024)}, u32[]{:S(2)}) copy-start(f32[1024]{0:T(1024)} %param.15) | copy-start | bytes 12292
  41.2 17.2 %copy-start.4 = (f32[8,1,20,1024]{3,2,0,1:T(8,128)S(1)}, f32[8,1,20,1024]{3,2,0,1:T(8,128)}, u32[]{:S(2)}) copy-start(f32[8,1,20,1024]{3,2,0,1:T(8,128)} %get-tuple-element.67) | copy-start | bytes 1966084
  41.2 17.8 %copy-start.2 = (bf16[16,20,1024]{2,1,0:T(8,128)(2,1)S(1)}, bf16[16,20,1024]{2,1,0:T(8,128)(2,1)}, u32[]{:S(2)}) copy-start(bf16[16,20,1024]{2,1,0:T(8,128)(2,1)} %copy-done.1) | copy-start | bytes 1966084
  41.2 154.3 %all-reduce.7.cloned.1.call-start = ((), (), s32[]{:S(2)}) async-start(), calls=%async_computation.1 | async-start | bytes 2293760 | tf_op jit(solution)/shard_map/psum | solution.py:99
  46.4 28.8 %copy-start.11 = (f32[3584]{0:T(1024)S(1)}, f32[3584]{0:T(1024)}, u32[]{:S(2)}) copy-start(f32[3584]{0:T(1024)} %param.14) | copy-start | bytes 43012
  46.4 28.9 %copy-start.9 = (f32[3584]{0:T(1024)S(1)}, f32[3584]{0:T(1024)}, u32[]{:S(2)}) copy-start(f32[3584]{0:T(1024)} %param.13) | copy-start | bytes 43012
  58.3 0.6 copy-start.14
  74.5 0.9 copy-start.7
  75.3 7.3 %copy-start.5 = (bf16[160,1024]{1,0:T(8,128)(2,1)}, bf16[160,1024]{1,0:T(8,128)(2,1)S(1)}, u32[]{:S(2)}) copy-start(bf16[160,1024]{1,0:T(8,128)(2,1)S(1)} %multiply_convert_fusion.4) | copy-start | bytes 983044
  75.3 7.3 %copy-start.17 = (f32[160]{0:T(256)S(1)}, f32[160]{0:T(256)}, u32[]{:S(2)}) copy-start(f32[160]{0:T(256)} %sub.98) | copy-start | bytes 1924
  146.0 17.8 %copy-start.15 = (f32[1024]{0:T(1024)S(1)}, f32[1024]{0:T(1024)}, u32[]{:S(2)}) copy-start(f32[1024]{0:T(1024)} %copy-done.14) | copy-start | bytes 12292
  146.0 18.4 %copy-start.3 = (bf16[160,3584]{1,0:T(8,128)(2,1)S(1)}, bf16[160,3584]{1,0:T(8,128)(2,1)}, u32[]{:S(2)}) copy-start(bf16[160,3584]{1,0:T(8,128)(2,1)} %get-tuple-element.59) | copy-start | bytes 3440644
  146.0 18.4 %copy-start.6 = (bf16[160,1024]{1,0:T(8,128)(2,1)S(1)}, bf16[160,1024]{1,0:T(8,128)(2,1)}, u32[]{:S(2)}) copy-start(bf16[160,1024]{1,0:T(8,128)(2,1)} %copy-done.5) | copy-start | bytes 983044
  175.3 21.8 %copy-start.16 = (f32[160]{0:T(256)S(1)}, f32[160]{0:T(256)}, u32[]{:S(2)}) copy-start(f32[160]{0:T(256)} %slice_reduce_fusion.4) | copy-start | bytes 1924
  195.5 11.7 %slice-start = ((s8[7340032]{0:T(1024)(128)(4,1)}), s8[4194304]{0:T(1024)(128)(4,1)S(1)}, s32[]{:S(2)}) async-start(s8[7340032]{0:T(1024)(128)(4,1)} %bitcast.42), calls=%async_computation.3 | async-start | bytes 8388608
  197.1 10.0 %slice-start.1 = ((s8[7340032]{0:T(1024)(128)(4,1)}), s8[3145728]{0:T(1024)(128)(4,1)S(1)}, s32[]{:S(2)}) async-start(s8[7340032]{0:T(1024)(128)(4,1)} %bitcast.42), calls=%async_computation.4 | async-start | bytes 6291456
  207.2 9.2 %copy-start.10 = (f32[3584]{0:T(1024)S(1)}, f32[3584]{0:T(1024)}, u32[]{:S(2)}) copy-start(f32[3584]{0:T(1024)} %param.13) | copy-start | bytes 43012
  207.2 9.2 %copy-start.12 = (f32[3584]{0:T(1024)S(1)}, f32[3584]{0:T(1024)}, u32[]{:S(2)}) copy-start(f32[3584]{0:T(1024)} %param.14) | copy-start | bytes 43012
  212.2 23.6 %all-to-all-start = ((bf16[8,20,1024]{2,1,0:T(8,128)(2,1)}), bf16[8,20,1024]{2,1,0:T(8,128)(2,1)S(1)}, u32[]{:S(2)}, u32[]{:S(2)}) async-start(bf16[8,20,1024]{2,1,0:T(8,128)(2,1)} %reshape.123), calls=%async_computation | async-start | bytes 786432 | tf_op jit(solution)/shard_map/all_to_all | solution.py:140
  217.0 11.0 %slice-start.4 = ((s8[7340032]{0:T(1024)(128)(4,1)}), s8[4194304]{0:T(1024)(128)(4,1)S(1)}, s32[]{:S(2)}) async-start(s8[7340032]{0:T(1024)(128)(4,1)} %bitcast.46), calls=%async_computation.7 | async-start | bytes 8388608
  217.0 11.0 %slice-start.5 = ((s8[7340032]{0:T(1024)(128)(4,1)}), s8[3145728]{0:T(1024)(128)(4,1)S(1)}, s32[]{:S(2)}) async-start(s8[7340032]{0:T(1024)(128)(4,1)} %bitcast.46), calls=%async_computation.8 | async-start | bytes 6291456
  228.0 8.0 %copy-start.8 = (bf16[20,1024]{1,0:T(8,128)(2,1)S(1)}, bf16[20,1024]{1,0:T(8,128)(2,1)}, u32[]{:S(2)}) copy-start(bf16[20,1024]{1,0:T(8,128)(2,1)} %param.9) | copy-start | bytes 122884
Sparse Core Ops, SparseCore 0:
  41.3 97.4 all-reduce.8
  141.3 54.1 all-reduce.6
